TPU v7x, 256 devices: a whole 4x4x8 slice. The times are simulated.
256 devices in a mesh: band: 64 (over y, z, core), grp: 4 (over x).
Axes of the slice: x: 4, y: 4, z: 8, core: 2. Of those that a mesh axis runs over, the one named last changes fastest.
Arguments:
- coarse: bfloat16 [64, 60, 73, 384], P('band', 'grp'), may hold values from -6 to 6
- region_lat: int32 [12], replicated, may hold values from 0 to 62
- region_lon: int32 [12], replicated, may hold values from 0 to 59
- region_order: int32 [12], replicated, may hold values from 0 to 11, each once
- conv_weight: bfloat16 [9, 128, 73], replicated, may hold values from -0.25 to 0.25
- conv_bias: float32 [128], replicated, may hold values from -3 to 3
Outputs:
- tiles: bfloat16 [12, 64, 128, 3136], P('grp', 'band')
All inputs are finite; a program needn't handle non-finite values.
Results may differ from a plain program's by a relative error of at most 0.0042.
Values may be sent and summed in bfloat16 or wider, within the bound.
No kernel may reach another device: no remote copies, remote signals or barrier semaphores. Data moves between devices by JAX's collectives and lax.ppermute only.
A program may use at most 64 MiB of HBM per device.

v0:
```python
import functools

import jax
import jax.numpy as jnp
from jax import lax
from jax.experimental import pallas as pl
from jax.experimental.layout import Layout, with_layout_constraint
from jax.experimental.pallas import tpu as pltpu
from jax.sharding import PartitionSpec as P

CH = 73
CO = 128
FN = 448
BR = 16
BC = 24
CELLS = BR * BC
TCOLS = 8
TH = 56
TW = 56
WR = 6
WC = 8
MAIN = 64
REST = CH - MAIN
ROW = 64
NEAR = 3
DEPTH = 256
UROWS = 14
CAPACITIES = (1, 2, 3, 4, 12)
F32 = jnp.float32
BF16 = jnp.bfloat16


def bilinear(positions, node_count, fine_count, nodes):
    coords = (positions.astype(F32) + 0.5) * (node_count / fine_count) - 0.5
    coords = jnp.clip(coords, 0.0, node_count - 1.0)
    weight = jnp.maximum(0.0, 1.0 - jnp.abs(coords - nodes.astype(F32)))
    inside = (positions >= 0) & (positions < fine_count)
    return jnp.where(inside, weight, 0.0)


def plan_kernel(lat, lon, order, table, chips, places, branch, counts):
    band, group = lax.axis_index("band"), lax.axis_index("grp")
    chip, core = lax.shift_right_logical(band, 1), lax.bitwise_and(band, 1)
    spot = lax.broadcasted_iota(jnp.int32, (8, 128), 1)
    spot_m, spot_g = lax.bitwise_and(spot, 31), lax.shift_right_logical(spot, 5)
    tally = jnp.zeros((8, 128), jnp.int32)
    for n in range(48):
        table[n] = -1
    held = []
    for i in range(12):
        region = order[i]
        lat0, lon0 = lat[region], lon[region]
        lon1 = jnp.where(lon0 == 59, 0, lon0 + 1)
        m0, m1 = lax.shift_right_logical(lat0, 1), lax.shift_right_logical(lat0 + 1, 1)
        g0, g1 = [
            (x >= 15).astype(jnp.int32) + (x >= 30).astype(jnp.int32) + (x >= 45).astype(jnp.int32)
            for x in (lon0, lon1)
        ]
        meets = ((spot_m == m0) | (spot_m == m1)) & ((spot_g == g0) | (spot_g == g1))
        tally = tally + meets.astype(jnp.int32)
        counts[m0] = 0
        counts[m1] = 0
        chips[2 * i] = m0
        chips[2 * i + 1] = m1
        held.append((lat0, lon0, lon1, m0, m1, (g0 == group) | (g1 == group)))
    counts[chip] = 0
    for i, (lat0, lon0, lon1, m0, m1, here) in enumerate(held):
        one = here.astype(jnp.int32)
        two = (here & (m0 != m1)).astype(jnp.int32)
        q = counts[chip]
        n0 = counts[m0]
        places[2 * i] = jnp.where(here, n0, -1)
        counts[m0] = n0 + one
        n1 = counts[m1]
        places[2 * i + 1] = jnp.where(two == 1, n1, -1)
        counts[m1] = n1 + two

        @pl.when(here & ((m0 == chip) | (m1 == chip)))
        def _():
            for j in range(2):
                row = lat0 + j - 2 * chip
                for k, at in enumerate((lon0, lon1)):
                    col = at - 15 * group
                    ok = (row >= 0) & (row < 2) & (col >= 0) & (col < 15)
                    side = jnp.where(row == core, 0, 16)
                    table[q * 4 + j * 2 + k] = jnp.where(ok, side + col, -1)

    most = jnp.max(tally)
    step = jnp.int32(0)
    for cap in CAPACITIES[:-1]:
        step = step + (most > cap).astype(jnp.int32)
    branch[0] = step


def plan(lat, lon, order):
    smem = pl.BlockSpec(memory_space=pltpu.SMEM)
    return pl.pallas_call(
        plan_kernel,
        out_shape=[jax.ShapeDtypeStruct((n,), jnp.int32) for n in (48, 24, 24, 1)],
        in_specs=[smem] * 3,
        out_specs=[smem] * 4,
        scratch_shapes=[pltpu.SMEM((33,), jnp.int32)],
        name="plan",
    )(lat, lon, order)


def payload_rows(capacity):
    return 24 * capacity + 8 * ((capacity + 1) // 2)


def pick_kernel(capacity, table, own, other, out, window, blocks):
    core = lax.rem(lax.axis_index("band"), 2)
    lane = lax.broadcasted_iota(jnp.int32, (8, 128), 1)
    turn = (
        lax.broadcasted_iota(jnp.int32, (128, 128), 0)
        == lax.broadcasted_iota(jnp.int32, (128, 128), 1)
    ).astype(BF16)
    zeros = jnp.zeros((ROW, 128), F32)
    for n in range(4 * capacity):
        code = table[n]

        @pl.when(code < 0)
        def _():
            blocks[n * 128 : (n + 1) * 128] = jnp.zeros((128, CELLS), BF16)

        @pl.when((code >= 0) & (code < 16))
        def _():
            blocks[n * 128 : n * 128 + CH] = own[code]

        @pl.when(code >= 16)
        def _():
            blocks[n * 128 : n * 128 + CH] = other[code - 16]

    for q in range(capacity):
        base = q * 34 * ROW
        window[base : base + ROW] = zeros
        window[base + 33 * ROW : base + 34 * ROW] = zeros
        for r in range(1, 33):
            window[base + r * ROW : base + r * ROW + 8] = zeros[:8]
            window[base + r * ROW + 56 : base + r * ROW + 64] = zeros[:8]
        turned = jnp.concatenate(
            [
                lax.dot_general(
                    turn,
                    blocks[512 * q : 512 * q + 512, 128 * i : 128 * i + 128],
                    (((1,), (1,)), ((), ())),
                    preferred_element_type=F32,
                )
                for i in range(3)
            ],
            axis=0,
        )
        for j in range(2):
            for k in range(2):
                n = 2 * j + k
                for r in range(BR):
                    at = base + (16 * j + r + 1) * ROW + 8 + BC * k
                    window[at : at + BC] = turned[
                        r * BC : (r + 1) * BC, n * 128 : (n + 1) * 128
                    ]

    def emit(a, carry):
        for b in range(4):
            mains, rests = [], []
            for q in range(capacity):
                rows = []
                for i in range(WR):
                    at = q * 34 * ROW + i * ROW + 7 + 12 * b + 6 * core + a * 4 * ROW
                    rows.append(window[pl.ds(at, WC)])
                for i in range(3):
                    mains.append(
                        jnp.where(lane < MAIN, rows[i], pltpu.roll(rows[i + 3], MAIN, 1))
                    )
                side = 64 * (q % 2)
                rest = jnp.zeros((8, 128), F32)
                for i in range(WR):
                    lo = side + REST * i
                    moved = pltpu.roll(rows[i], (lo - MAIN) % 128, 1)
                    rest = jnp.where((lane >= lo) & (lane < lo + REST), moved, rest)
                if q % 2 == 0:
                    rests.append(rest)
                else:
                    rests[-1] = rests[-1] + rest
            out[4 * a + b] = jnp.concatenate(mains + rests, axis=0).astype(BF16)
        return carry

    lax.fori_loop(0, 8, emit, 0, unroll=8 if capacity <= 2 else 1)


def pick(capacity, table, own, other):
    vmem = pl.BlockSpec(memory_space=pltpu.VMEM)
    smem = pl.BlockSpec(memory_space=pltpu.SMEM)
    return pl.pallas_call(
        functools.partial(pick_kernel, capacity),
        out_shape=jax.ShapeDtypeStruct((32, payload_rows(capacity), 128), BF16),
        in_specs=[smem, vmem, vmem],
        out_specs=vmem,
        scratch_shapes=[
            pltpu.VMEM((capacity * 34 * ROW, 128), F32),
            pltpu.VMEM((capacity * 4 * 128, CELLS), BF16),
        ],
        compiler_params=pltpu.CompilerParams(vmem_limit_bytes=40 * 2**20),
        name="pick",
    )(table, own, other)


def regroup_kernel(capacity, chips, places, got, *outs):
    group = lax.axis_index("grp")
    lane = lax.broadcasted_iota(jnp.int32, (8, 128), 1)
    def gather(out, hop, s):
        slot = lax.bitwise_and(group + hop, 3) * 3 + s
        main = jnp.zeros((24, 128), F32)
        rest = jnp.zeros((8, 128), F32)
        for j in range(2):
            place = places[slot * 2 + j]
            part = got[chips[slot * 2 + j]].astype(F32)
            for q in range(capacity):
                here = place == q
                main = main + jnp.where(here, part[24 * q : 24 * q + 24], 0.0)
                at = 24 * capacity + 8 * (q // 2)
                side = part[at : at + 8]
                if q % 2:
                    side = pltpu.roll(side, 64, 1)
                rest = rest + jnp.where(here, side, 0.0)
        rows = []
        for i in range(WR):
            body = main[8 * (i % 3) : 8 * (i % 3) + 8]
            if i >= 3:
                body = pltpu.roll(body, 64, 1)
            tail = pltpu.roll(rest, (MAIN - REST * i) % 128, 1)
            row = jnp.where(lane < MAIN, body, jnp.where(lane < CH, tail, 0.0))
            rows.append(row)
        out[WR * WC * s : WR * WC * (s + 1)] = jnp.concatenate(rows, axis=0).astype(BF16)

    for hop in range(4):
        for s in range(3):
            gather(outs[hop], hop, s)


def regroup(capacity, chips, places, got):
    vmem = pl.BlockSpec(memory_space=pltpu.VMEM)
    smem = pl.BlockSpec(memory_space=pltpu.SMEM)
    return pl.pallas_call(
        functools.partial(regroup_kernel, capacity),
        out_shape=[jax.ShapeDtypeStruct((3 * WR * WC, 128), BF16)] * 4,
        in_specs=[smem, smem, vmem],
        out_specs=[vmem] * 4,
        compiler_params=pltpu.CompilerParams(vmem_limit_bytes=24 * 2**20),
        name="regroup",
    )(chips, places, got)


def conv_kernel(win0, win1, win2, win3, weight, bias, row_part, col_part, out, taps):
    step = pl.program_id(0)
    n = WR * WC

    @pl.when(step == 0)
    def _():
        cells = win0[...].astype(F32) + win1[...].astype(F32)
        cells = cells + (win2[...].astype(F32) + win3[...].astype(F32))
        cells = cells.astype(BF16)[:, :CH]
        every = jnp.concatenate([weight[t] for t in range(9)], axis=1)
        made = jnp.dot(cells, every, preferred_element_type=F32) * 0.5
        for t in range(9):
            for s in range(3):
                taps[t * n : (t + 1) * n, s * CO : (s + 1) * CO] = made[
                    s * n : (s + 1) * n, t * CO : (t + 1) * CO
                ]

    near = [
        taps[pl.ds(pl.multiple_of(t * n + WC * step, 8), NEAR * WC)] for t in range(9)
    ]
    near.append(jnp.zeros((DEPTH - 9 * NEAR * WC, 3 * CO), F32))
    near = jnp.concatenate(near, axis=0).astype(BF16)
    cols = col_part[...]
    spread = jnp.concatenate(
        [cols * row_part[pl.ds(step * UROWS + u, 1)] for u in range(UROWS)], axis=0
    ).astype(BF16)
    half = jnp.dot(spread, near, preferred_element_type=F32)
    for s in range(3):
        h = half[:, s * CO : (s + 1) * CO] + 0.5 * bias[...]
        out[s, 0] = (h + h * jnp.tanh(h)).astype(BF16)


def convolve(wins, weight, bias, row_part, col_part):
    whole = pl.BlockSpec(memory_space=pltpu.VMEM)
    return pl.pallas_call(
        conv_kernel,
        grid=(TH // UROWS,),
        out_shape=jax.ShapeDtypeStruct((3, 1, TH * TW, CO), BF16),
        in_specs=[whole] * 8,
        out_specs=pl.BlockSpec((3, 1, UROWS * TW, CO), lambda i: (0, 0, i, 0)),
        scratch_shapes=[pltpu.VMEM((9 * WR * WC, 3 * CO), F32)],
        compiler_params=pltpu.CompilerParams(vmem_limit_bytes=40 * 2**20),
        name="convolve",
    )(*wins, weight, bias, row_part, col_part)


def spread_parts(tile_row, tile_col):
    lane = jnp.arange(DEPTH, dtype=jnp.int32)[None, :]
    pixel = jnp.arange(TH, dtype=jnp.int32)[:, None]
    row_pos = tile_row * TH - 1 + lane // (3 * NEAR * WC) + pixel
    row_node = 4 * tile_row - 1 + pixel // UROWS + (lane // WC) % NEAR
    col_pos = tile_col * TW - 1 + (lane // (NEAR * WC)) % 3 + pixel
    col_node = 6 * tile_col - 1 + lane % WC
    rows = bilinear(row_pos, 2 * BR, FN, row_node)
    cols = bilinear(col_pos, 2 * BC, FN, col_node)
    return rows, cols


def on_device(coarse, region_lat, region_lon, region_order, conv_weight, conv_bias):
    band = lax.axis_index("band")
    own = coarse[0]
    other = lax.ppermute(own, "band", [(i, i ^ 1) for i in range(64)])
    table, chips, places, branch = plan(region_lat, region_lon, region_order)
    branch = jnp.clip(branch[0], 0, len(CAPACITIES) - 1)
    own, table, branch = lax.optimization_barrier((own, table, branch))
    own = with_layout_constraint(own, Layout(major_to_minor=(0, 1, 2)))
    planes = [[2 * m + c for m in range(32)] for c in range(2)]

    def route(capacity):
        def run(own, other, table, chips, places):
            cut = pick(capacity, table, own, other)
            got = lax.all_to_all(cut, "band", 0, 0, axis_index_groups=planes)
            return regroup(capacity, chips, places, got)

        return run

    tiles = lax.switch(
        branch, [route(cap) for cap in CAPACITIES], own, other, table, chips, places
    )
    band, *tiles = lax.optimization_barrier((band, *tiles))
    wins = [tiles[0]] + [
        lax.ppermute(tiles[hop], "grp", [(i, (i + hop) % 4) for i in range(4)])
        for hop in (2, 1, 3)
    ]
    rows, cols = spread_parts(band // TCOLS, band % TCOLS)
    weight = jnp.swapaxes(conv_weight, 1, 2)
    return jnp.swapaxes(convolve(wins, weight, conv_bias[None, :], rows, cols), 2, 3)


def solution(mesh):
    in_specs = (P("band", "grp", None, None), P(), P(), P(), P(), P())
    out_specs = P("grp", "band", None, None)
    return jax.shard_map(
        on_device, mesh=mesh, in_specs=in_specs, out_specs=out_specs, check_vma=False
    )
```

profile of v0, /device:TPU:6, one launch (start us, length us, event | category | flops | bytes accessed | tf_op | source)
XLA Modules:
  0.0 46.0 jit_solution(17223634702920863605)
XLA Ops:
  0.0 0.0 collective-permute-start
  0.0 1.4 %copy.17 = bf16[1,15,73,384]{3,2,1,0:T(8,128)(2,1)S(1)} copy(bf16[1,15,73,384]{3,1,2,0:T(8,128)(2,1)} %param.11) | data formatting | bytes 1681920 | tf_op args[0]
  1.4 1.8 %plan.1 = (s32[48]{0:T(128)S(1)}, s32[24]{0:T(128)S(1)}, s32[24]{0:T(128)S(1)}, s32[1]{0:T(128)}) custom-call(s32[12]{0:T(128)} %lat.1, s32[12]{0:T(128)} %lon.1, s32[12]{0:T(128)} %order.1), custom_call_target="tpu_custom_call" | custom-call | tf_op jit(solution)/shard_map/plan/pallas_call | solution.py:97
  3.8 0.0 collective-permute-done
  3.8 0.0 copy-start
  3.8 0.0 copy-start.1
  3.8 30.3 %conditional.1 = ((bf16[144,128]{1,0:T(8,128)(2,1)S(1)}, bf16[144,128]{1,0:T(8,128)(2,1)S(1)}, bf16[144,128]{1,0:T(8,128)(2,1)S(1)}, bf16[144,128]{1,0:T(8,128)(2,1)S(1)})) conditional(s32[]{:T(128)} %clamp.5, (s32[48]{0:T(128)S(1)}, bf16[15,73,384]{2,1,0:T(8,128)(2,1)S(1)}, bf16[15,73,384]{2,0,1:T(8,128)(2,1)S(1)}, ...), branch_computations={%region_0.1_spmd, %region_1.2_spmd, %region_2.3_spmd, %region_3.4_... | conditional | bytes 7186952 | solution.py:329
  3.9 0.2 copy.11.other
  4.1 1.6 %pick.6 = bf16[32,56,128]{2,1,0:T(8,128)(2,1)S(1)} custom-call(s32[48]{0:T(128)S(1)} %get-tuple-element.62.table, bf16[15,73,384]{2,1,0:T(8,128)(2,1)S(1)} %get-tuple-element.63.own, bf16[15,73,384]{2,1,0:T(8,128)(2,1)S(1)} %copy.11.other), custom_call_target="tpu_custom_call" | custom-call | tf_op jit(solution)/shard_map/cond/branch_1_fun/pick/pallas_call | solution.py:193
  5.7 27.4 %all_to_all.21.got = bf16[32,56,128]{2,1,0:T(8,128)(2,1)S(1)} all-to-all(bf16[32,56,128]{2,1,0:T(8,128)(2,1)S(1)} %pick.6), channel_id=1, replica_groups={{0,8,16,24,32,40,48,56,64,72,80,88,96,104,112,120,128,136,144,152,160,1..., dimensions={0} | all-to-all | bytes 917504 | tf_op jit(solution)/shard_map/cond/branch_1_fun/all_to_all | solution.py:324
  33.1 0.8 %regroup.6 = (bf16[144,128]{1,0:T(8,128)(2,1)S(1)}, bf16[144,128]{1,0:T(8,128)(2,1)S(1)}, bf16[144,128]{1,0:T(8,128)(2,1)S(1)}, bf16[144,128]{1,0:T(8,128)(2,1)S(1)}) custom-call(s32[24]{0:T(128)S(1)} %get-tuple-element.60.chips, s32[24]{0:T(128)S(1)} %get-tuple-element.61.places, bf16[32,56,128]{2,1,0:T(8,128)(2,1)S(1)} %all_to_all.21.got), custom_call_target="tpu_custom_call" | custom-call | tf_op jit(solution)/shard_map/cond/branch_1_fun/regroup/pallas_call | solution.py:243
  34.2 1.5 %collective-permute-start.1 = (bf16[144,128]{1,0:T(8,128)(2,1)S(1)}, bf16[144,128]{1,0:T(8,128)(2,1)S(1)}, u32[]{:S(2)}, u32[]{:S(2)}) collective-permute-start(bf16[144,128]{1,0:T(8,128)(2,1)S(1)} %get-tuple-element.108), channel_id=1, source_target_pairs={{0,2},{1,3},{2,0},{3,1},{4,6},{5,7},{6,4},{7,5},{8,10},{9,11},{10,... | collective-permute-start | bytes 110600 | tf_op jit(solution)/shard_map/ppermute | solution.py:334
  35.7 2.1 %collective-permute-start.2 = (bf16[144,128]{1,0:T(8,128)(2,1)S(1)}, bf16[144,128]{1,0:T(8,128)(2,1)S(1)}, u32[]{:S(2)}, u32[]{:S(2)}) collective-permute-start(bf16[144,128]{1,0:T(8,128)(2,1)S(1)} %get-tuple-element.109), channel_id=1, source_target_pairs={{0,1},{1,2},{2,3},{3,0},{4,5},{5,6},{6,7},{7,4},{8,9},{9,10},{10,1... | collective-permute-start | bytes 110600 | tf_op jit(solution)/shard_map/ppermute | solution.py:334
  37.8 0.0 collective-permute-start.3
  37.8 0.1 maximum_select_fusion.1.row_part
  38.0 1.9 %collective-permute-done.1.win1 = bf16[144,128]{1,0:T(8,128)(2,1)S(1)} collective-permute-done((bf16[144,128]{1,0:T(8,128)(2,1)S(1)}, bf16[144,128]{1,0:T(8,128)(2,1)S(1)}, u32[]{:S(2)}, u32[]{:S(2)}) %collective-permute-start.1) | collective-permute-done | bytes 36896 | tf_op jit(solution)/shard_map/ppermute | solution.py:334
  39.9 0.0 collective-permute-done.2.win2
  39.9 3.1 %collective-permute-done.3.win3 = bf16[144,128]{1,0:T(8,128)(2,1)S(1)} collective-permute-done((bf16[144,128]{1,0:T(8,128)(2,1)S(1)}, bf16[144,128]{1,0:T(8,128)(2,1)S(1)}, u32[]{:S(2)}, u32[]{:S(2)}) %collective-permute-start.3) | collective-permute-done | bytes 36896 | tf_op jit(solution)/shard_map/ppermute | solution.py:334
  43.0 0.0 copy-done
  43.0 0.0 copy-done.1
  43.0 3.1 %convolve.1 = bf16[3,1,3136,128]{3,2,1,0:T(8,128)(2,1)} custom-call(bf16[144,128]{1,0:T(8,128)(2,1)S(1)} %get-tuple-element.107.win0, bf16[144,128]{1,0:T(8,128)(2,1)S(1)} %collective-permute-done.1.win1, bf16[144,128]{1,0:T(8,128)(2,1)S(1)} %collective-permute-done.2.win2, bf16[144,128]{1,0:T(8,128)(2,1)S(1)} %collective-permute-done.3.win3, ...), custom_call_target="tpu_custom_call" | custom-call | tf_op jit(solution)/shard_map/convolve/pallas_call | solution.py:287
  (4 shorter events, 0.1 us)
Async XLA Ops:
  0.0 3.8 %collective-permute-start = (bf16[15,73,384]{2,0,1:T(8,128)(2,1)}, bf16[15,73,384]{2,0,1:T(8,128)(2,1)S(1)}, u32[]{:S(2)}, u32[]{:S(2)}) collective-permute-start(bf16[15,73,384]{2,0,1:T(8,128)(2,1)} %bitcast.15), channel_id=1, source_target_pairs={{0,4},{4,0},{8,12},{12,8},{16,20},{20,16},{24,28},{28,24},{32,36},... | collective-permute-start | bytes 2522888 | tf_op jit(solution)/shard_map/ppermute | solution.py:314
  3.8 39.2 %copy-start = (bf16[9,128,73]{1,2,0:T(8,128)(2,1)S(1)}, bf16[9,128,73]{1,2,0:T(8,128)(2,1)}, u32[]{:S(2)}) copy-start(bf16[9,128,73]{1,2,0:T(8,128)(2,1)} %param.15) | copy-start | bytes 504580
  3.8 39.2 %copy-start.1 = (f32[128]{0:T(128)S(1)}, f32[128]{0:T(128)}, u32[]{:S(2)}) copy-start(f32[128]{0:T(128)} %param.16) | copy-start | bytes 1540
  34.2 5.6 %collective-permute-start.1 = (bf16[144,128]{1,0:T(8,128)(2,1)S(1)}, bf16[144,128]{1,0:T(8,128)(2,1)S(1)}, u32[]{:S(2)}, u32[]{:S(2)}) collective-permute-start(bf16[144,128]{1,0:T(8,128)(2,1)S(1)} %get-tuple-element.108), channel_id=1, source_target_pairs={{0,2},{1,3},{2,0},{3,1},{4,6},{5,7},{6,4},{7,5},{8,10},{9,11},{10,... | collective-permute-start | bytes 110600 | tf_op jit(solution)/shard_map/ppermute | solution.py:334
  35.7 4.1 %collective-permute-start.2 = (bf16[144,128]{1,0:T(8,128)(2,1)S(1)}, bf16[144,128]{1,0:T(8,128)(2,1)S(1)}, u32[]{:S(2)}, u32[]{:S(2)}) collective-permute-start(bf16[144,128]{1,0:T(8,128)(2,1)S(1)} %get-tuple-element.109), channel_id=1, source_target_pairs={{0,1},{1,2},{2,3},{3,0},{4,5},{5,6},{6,7},{7,4},{8,9},{9,10},{10,1... | collective-permute-start | bytes 110600 | tf_op jit(solution)/shard_map/ppermute | solution.py:334
  37.8 5.2 %collective-permute-start.3 = (bf16[144,128]{1,0:T(8,128)(2,1)S(1)}, bf16[144,128]{1,0:T(8,128)(2,1)S(1)}, u32[]{:S(2)}, u32[]{:S(2)}) collective-permute-start(bf16[144,128]{1,0:T(8,128)(2,1)S(1)} %get-tuple-element.110), channel_id=1, source_target_pairs={{0,3},{1,0},{2,1},{3,2},{4,7},{5,4},{6,5},{7,6},{8,11},{9,8},{10,9... | collective-permute-start | bytes 110600 | tf_op jit(solution)/shard_map/ppermute | solution.py:334
where the time goes:
time: 46.8 us; the launch traced here: 46 us
  blocking collectives  27.4 us (59%)
  Pallas kernels  7.26 us (16%)
  waiting for transfers between devices  5.01 us (11%)
  starting transfers between devices  3.59 us (8%)
  local copies, waits for them, and re-layouts  1.57 us (3%)
  between operations  0.76 us (2%)
    all_to_all x1, blocking collectives, run(): got = lax.all_to_all(cut, 'band', 0, 0, axis_index_groups=planes)  27.4 us
    ppermute x3, waiting for transfers between devices, on_device(): lax.ppermute(tiles[hop], 'grp', [(i, (i + hop) % 4) for i in range(4)])  5.01 us
    ppermute x3, starting transfers between devices, on_device(): lax.ppermute(tiles[hop], 'grp', [(i, (i + hop) % 4) for i in range(4)])  3.59 us
    pallas_call x1, Pallas kernels, convolve(): pl.pallas_call(conv_kernel, grid=(TH // UROWS,), out_shape=jax.ShapeDtype...  3.05 us
    pallas_call x1, Pallas kernels, plan(): pl.pallas_call(plan_kernel, out_shape=[jax.ShapeDtypeStruct((n,), jnp.int...  1.77 us
    pallas_call x1, Pallas kernels, pick(): pl.pallas_call(functools.partial(pick_kernel, capacity), out_shape=jax.Sh...  1.65 us
    unnamed x5, local copies, waits for them, and re-layouts  1.38 us
  transfers between devices with their start and end apart: 4, of which 2 were waited for; matrix products, arithmetic and copies ran while one was open for 3% of the time, Pallas kernels for 4%

commit v1 on v0

--- a/solution.py
+++ b/solution.py
@@ -25,6 +25,10 @@
 NEAR = 3
 DEPTH = 256
 UROWS = 14
+SPARE = 48
+CHIPS = 56
+PLACES = 80
+HELD = 104
 CAPACITIES = (1, 2, 3, 4, 12)
 F32 = jnp.float32
 BF16 = jnp.bfloat16
@@ -38,14 +42,12 @@
     return jnp.where(inside, weight, 0.0)
 
 
-def plan_kernel(lat, lon, order, table, chips, places, branch, counts):
+def plan_kernel(lat, lon, order, tables, branch, counts):
     band, group = lax.axis_index("band"), lax.axis_index("grp")
     chip, core = lax.shift_right_logical(band, 1), lax.bitwise_and(band, 1)
     spot = lax.broadcasted_iota(jnp.int32, (8, 128), 1)
     spot_m, spot_g = lax.bitwise_and(spot, 31), lax.shift_right_logical(spot, 5)
     tally = jnp.zeros((8, 128), jnp.int32)
-    for n in range(48):
-        table[n] = -1
     held = []
     for i in range(12):
         region = order[i]
@@ -60,45 +62,44 @@
         tally = tally + meets.astype(jnp.int32)
         counts[m0] = 0
         counts[m1] = 0
-        chips[2 * i] = m0
-        chips[2 * i + 1] = m1
+        tables[CHIPS + 2 * i] = m0
+        tables[CHIPS + 2 * i + 1] = m1
         held.append((lat0, lon0, lon1, m0, m1, (g0 == group) | (g1 == group)))
-    counts[chip] = 0
-    for i, (lat0, lon0, lon1, m0, m1, here) in enumerate(held):
-        one = here.astype(jnp.int32)
-        two = (here & (m0 != m1)).astype(jnp.int32)
-        q = counts[chip]
-        n0 = counts[m0]
-        places[2 * i] = jnp.where(here, n0, -1)
-        counts[m0] = n0 + one
-        n1 = counts[m1]
-        places[2 * i + 1] = jnp.where(two == 1, n1, -1)
-        counts[m1] = n1 + two
-
-        @pl.when(here & ((m0 == chip) | (m1 == chip)))
-        def _():
-            for j in range(2):
-                row = lat0 + j - 2 * chip
-                for k, at in enumerate((lon0, lon1)):
-                    col = at - 15 * group
-                    ok = (row >= 0) & (row < 2) & (col >= 0) & (col < 15)
-                    side = jnp.where(row == core, 0, 16)
-                    table[q * 4 + j * 2 + k] = jnp.where(ok, side + col, -1)
-
     most = jnp.max(tally)
     step = jnp.int32(0)
     for cap in CAPACITIES[:-1]:
         step = step + (most > cap).astype(jnp.int32)
     branch[0] = step
+    q = jnp.int32(0)
+    for i, (lat0, lon0, lon1, m0, m1, here) in enumerate(held):
+        one = here.astype(jnp.int32)
+        two = jnp.where(m0 != m1, one, 0)
+        n0 = counts[m0]
+        counts[m0] = n0 + one
+        n1 = counts[m1]
+        counts[m1] = n1 + two
+        tables[PLACES + 2 * i] = jnp.where(here, n0, -1)
+        tables[PLACES + 2 * i + 1] = jnp.where(two == 1, n1, -1)
+        mine = here & ((m0 == chip) | (m1 == chip))
+        at = jnp.where(mine, 4 * q, SPARE)
+        for j in range(2):
+            row = lat0 + j - 2 * chip
+            side = jnp.where(row == core, 0, 16)
+            for k, place in enumerate((lon0, lon1)):
+                col = place - 15 * group
+                ok = (row >= 0) & (row < 2) & (col >= 0) & (col < 15)
+                tables[at + 2 * j + k] = jnp.where(ok, side + col, -1)
+        q = q + mine.astype(jnp.int32)
+    tables[HELD] = q
 
 
 def plan(lat, lon, order):
     smem = pl.BlockSpec(memory_space=pltpu.SMEM)
     return pl.pallas_call(
         plan_kernel,
-        out_shape=[jax.ShapeDtypeStruct((n,), jnp.int32) for n in (48, 24, 24, 1)],
+        out_shape=[jax.ShapeDtypeStruct((n,), jnp.int32) for n in (128, 1)],
         in_specs=[smem] * 3,
-        out_specs=[smem] * 4,
+        out_specs=[smem] * 2,
         scratch_shapes=[pltpu.SMEM((33,), jnp.int32)],
         name="plan",
     )(lat, lon, order)
@@ -108,7 +109,7 @@
     return 24 * capacity + 8 * ((capacity + 1) // 2)
 
 
-def pick_kernel(capacity, table, own, other, out, window, blocks):
+def pick_kernel(capacity, tables, own, other, out, window, blocks):
     core = lax.rem(lax.axis_index("band"), 2)
     lane = lax.broadcasted_iota(jnp.int32, (8, 128), 1)
     turn = (
@@ -117,7 +118,7 @@
     ).astype(BF16)
     zeros = jnp.zeros((ROW, 128), F32)
     for n in range(4 * capacity):
-        code = table[n]
+        code = jnp.where(n // 4 < tables[HELD], tables[n], -1)
 
         @pl.when(code < 0)
         def _():
@@ -187,7 +188,7 @@
     lax.fori_loop(0, 8, emit, 0, unroll=8 if capacity <= 2 else 1)
 
 
-def pick(capacity, table, own, other):
+def pick(capacity, tables, own, other):
     vmem = pl.BlockSpec(memory_space=pltpu.VMEM)
     smem = pl.BlockSpec(memory_space=pltpu.SMEM)
     return pl.pallas_call(
@@ -201,10 +202,10 @@
         ],
         compiler_params=pltpu.CompilerParams(vmem_limit_bytes=40 * 2**20),
         name="pick",
-    )(table, own, other)
-
-
-def regroup_kernel(capacity, chips, places, got, *outs):
+    )(tables, own, other)
+
+
+def regroup_kernel(capacity, tables, got, *outs):
     group = lax.axis_index("grp")
     lane = lax.broadcasted_iota(jnp.int32, (8, 128), 1)
     def gather(out, hop, s):
@@ -212,8 +213,8 @@
         main = jnp.zeros((24, 128), F32)
         rest = jnp.zeros((8, 128), F32)
         for j in range(2):
-            place = places[slot * 2 + j]
-            part = got[chips[slot * 2 + j]].astype(F32)
+            place = tables[PLACES + slot * 2 + j]
+            part = got[tables[CHIPS + slot * 2 + j]].astype(F32)
             for q in range(capacity):
                 here = place == q
                 main = main + jnp.where(here, part[24 * q : 24 * q + 24], 0.0)
@@ -237,66 +238,72 @@
             gather(outs[hop], hop, s)
 
 
-def regroup(capacity, chips, places, got):
+def regroup(capacity, tables, got):
     vmem = pl.BlockSpec(memory_space=pltpu.VMEM)
     smem = pl.BlockSpec(memory_space=pltpu.SMEM)
     return pl.pallas_call(
         functools.partial(regroup_kernel, capacity),
         out_shape=[jax.ShapeDtypeStruct((3 * WR * WC, 128), BF16)] * 4,
-        in_specs=[smem, smem, vmem],
+        in_specs=[smem, vmem],
         out_specs=[vmem] * 4,
         compiler_params=pltpu.CompilerParams(vmem_limit_bytes=24 * 2**20),
         name="regroup",
-    )(chips, places, got)
-
-
-def conv_kernel(win0, win1, win2, win3, weight, bias, row_part, col_part, out, taps):
-    step = pl.program_id(0)
+    )(tables, got)
+
+
+def conv_kernel(win0, win1, win2, win3, weight, bias, spread, out, taps, result, sems):
     n = WR * WC
-
-    @pl.when(step == 0)
-    def _():
-        cells = win0[...].astype(F32) + win1[...].astype(F32)
-        cells = cells + (win2[...].astype(F32) + win3[...].astype(F32))
-        cells = cells.astype(BF16)[:, :CH]
-        every = jnp.concatenate([weight[t] for t in range(9)], axis=1)
-        made = jnp.dot(cells, every, preferred_element_type=F32) * 0.5
-        for t in range(9):
-            for s in range(3):
-                taps[t * n : (t + 1) * n, s * CO : (s + 1) * CO] = made[
-                    s * n : (s + 1) * n, t * CO : (t + 1) * CO
-                ]
-
-    near = [
-        taps[pl.ds(pl.multiple_of(t * n + WC * step, 8), NEAR * WC)] for t in range(9)
-    ]
-    near.append(jnp.zeros((DEPTH - 9 * NEAR * WC, 3 * CO), F32))
-    near = jnp.concatenate(near, axis=0).astype(BF16)
-    cols = col_part[...]
-    spread = jnp.concatenate(
-        [cols * row_part[pl.ds(step * UROWS + u, 1)] for u in range(UROWS)], axis=0
-    ).astype(BF16)
-    half = jnp.dot(spread, near, preferred_element_type=F32)
-    for s in range(3):
-        h = half[:, s * CO : (s + 1) * CO] + 0.5 * bias[...]
-        out[s, 0] = (h + h * jnp.tanh(h)).astype(BF16)
-
-
-def convolve(wins, weight, bias, row_part, col_part):
+    cells = win0[...].astype(F32) + win1[...].astype(F32)
+    cells = cells + (win2[...].astype(F32) + win3[...].astype(F32))
+    cells = cells.astype(BF16)[:, :CH]
+    every = jnp.concatenate([weight[t] for t in range(9)], axis=1)
+    made = jnp.dot(cells, every, preferred_element_type=F32) * 0.5
+    for t in range(9):
+        for s in range(3):
+            taps[t * n : (t + 1) * n, s * CO : (s + 1) * CO] = made[
+                s * n : (s + 1) * n, t * CO : (t + 1) * CO
+            ]
+    half_bias = 0.5 * bias[...]
+    size = UROWS * TW
+    sent = []
+    for step in range(TH // UROWS):
+        near = [
+            taps[t * n + WC * step : t * n + WC * (step + NEAR)] for t in range(9)
+        ]
+        near.append(jnp.zeros((DEPTH - 9 * NEAR * WC, 3 * CO), F32))
+        near = jnp.concatenate(near, axis=0).astype(BF16)
+        part = slice(step * size, (step + 1) * size)
+        half = jnp.dot(spread[part], near, preferred_element_type=F32)
+        for s in range(3):
+            h = half[:, s * CO : (s + 1) * CO] + half_bias
+            result[s, part] = (h + h * jnp.tanh(h)).astype(BF16)
+        rows = pl.ds(step * size, size)
+        sent.append(
+            pltpu.make_async_copy(result.at[:, rows], out.at[:, 0, rows], sems.at[step])
+        )
+        sent[-1].start()
+    for copy in sent:
+        copy.wait()
+
+
+def convolve(wins, weight, bias, spread):
     whole = pl.BlockSpec(memory_space=pltpu.VMEM)
     return pl.pallas_call(
         conv_kernel,
-        grid=(TH // UROWS,),
         out_shape=jax.ShapeDtypeStruct((3, 1, TH * TW, CO), BF16),
-        in_specs=[whole] * 8,
-        out_specs=pl.BlockSpec((3, 1, UROWS * TW, CO), lambda i: (0, 0, i, 0)),
-        scratch_shapes=[pltpu.VMEM((9 * WR * WC, 3 * CO), F32)],
+        in_specs=[whole] * 7,
+        out_specs=pl.BlockSpec(memory_space=pl.ANY),
+        scratch_shapes=[
+            pltpu.VMEM((9 * WR * WC, 3 * CO), F32),
+            pltpu.VMEM((3, TH * TW, CO), BF16),
+            pltpu.SemaphoreType.DMA((TH // UROWS,)),
+        ],
         compiler_params=pltpu.CompilerParams(vmem_limit_bytes=40 * 2**20),
         name="convolve",
-    )(*wins, weight, bias, row_part, col_part)
-
-
-def spread_parts(tile_row, tile_col):
+    )(*wins, weight, bias, spread)
+
+
+def spread_matrix(tile_row, tile_col):
     lane = jnp.arange(DEPTH, dtype=jnp.int32)[None, :]
     pixel = jnp.arange(TH, dtype=jnp.int32)[:, None]
     row_pos = tile_row * TH - 1 + lane // (3 * NEAR * WC) + pixel
@@ -305,38 +312,34 @@
     col_node = 6 * tile_col - 1 + lane % WC
     rows = bilinear(row_pos, 2 * BR, FN, row_node)
     cols = bilinear(col_pos, 2 * BC, FN, col_node)
-    return rows, cols
+    return (rows[:, None, :] * cols[None, :, :]).astype(BF16).reshape(TH * TW, DEPTH)
 
 
 def on_device(coarse, region_lat, region_lon, region_order, conv_weight, conv_bias):
     band = lax.axis_index("band")
     own = coarse[0]
     other = lax.ppermute(own, "band", [(i, i ^ 1) for i in range(64)])
-    table, chips, places, branch = plan(region_lat, region_lon, region_order)
-    branch = jnp.clip(branch[0], 0, len(CAPACITIES) - 1)
-    own, table, branch = lax.optimization_barrier((own, table, branch))
     own = with_layout_constraint(own, Layout(major_to_minor=(0, 1, 2)))
+    tables, branch = plan(region_lat, region_lon, region_order)
     planes = [[2 * m + c for m in range(32)] for c in range(2)]
 
     def route(capacity):
-        def run(own, other, table, chips, places):
-            cut = pick(capacity, table, own, other)
+        def run(own, other, tables):
+            cut = pick(capacity, tables, own, other)
             got = lax.all_to_all(cut, "band", 0, 0, axis_index_groups=planes)
-            return regroup(capacity, chips, places, got)
+            return regroup(capacity, tables, got)
 
         return run
 
-    tiles = lax.switch(
-        branch, [route(cap) for cap in CAPACITIES], own, other, table, chips, places
-    )
+    tiles = lax.switch(branch[0], [route(cap) for cap in CAPACITIES], own, other, tables)
     band, *tiles = lax.optimization_barrier((band, *tiles))
     wins = [tiles[0]] + [
         lax.ppermute(tiles[hop], "grp", [(i, (i + hop) % 4) for i in range(4)])
         for hop in (2, 1, 3)
     ]
-    rows, cols = spread_parts(band // TCOLS, band % TCOLS)
+    spread = spread_matrix(band // TCOLS, band % TCOLS)
     weight = jnp.swapaxes(conv_weight, 1, 2)
-    return jnp.swapaxes(convolve(wins, weight, conv_bias[None, :], rows, cols), 2, 3)
+    return jnp.swapaxes(convolve(wins, weight, conv_bias[None, :], spread), 2, 3)
 
 
 def solution(mesh):

time: 46.8 us -> 46 us (0.983)
  Pallas kernels: 7.26 us -> 6.27 us
  other arithmetic: 0.17 us -> 0.67 us
  waiting for transfers between devices: 5.01 us -> 4.51 us
    pallas_call x1, Pallas kernels: 3.05 us -> 2.06 us  [convolve(): pl.pallas_call(conv_kernel, out_shape=jax.ShapeDtypeStruct((3, 1, TH * TW...]
    ppermute x3, waiting for transfers between devices: 5.01 us -> 4.51 us  [on_device(): lax.ppermute(tiles[hop], 'grp', [(i, (i + hop) % 4) for i in range(4)])]
    convert_element_type x0 -> x1, other arithmetic: none -> 0.5 us  [spread_matrix(): (rows[:, None, :] * cols[None, :, :]).astype(BF16).reshape(TH * TW, DEPTH)]
  transfers between devices with their start and end apart: 4 -> 4, of which waited for: 2 -> 2; matrix products, arithmetic and copies ran while one was open for 3% -> 4% of each run, Pallas kernels for 4% -> 4%
where the time goes in v1:
time: 46 us; the launch traced here: 45.2 us
  blocking collectives  27.4 us (60%)
  Pallas kernels  6.27 us (14%)
  waiting for transfers between devices  4.51 us (10%)
  starting transfers between devices  3.59 us (8%)
  local copies, waits for them, and re-layouts  1.57 us (3%)
  between operations  0.94 us (2%)
  other arithmetic  0.67 us (1%)
    all_to_all x1, blocking collectives, run(): got = lax.all_to_all(cut, 'band', 0, 0, axis_index_groups=planes)  27.4 us
    ppermute x3, waiting for transfers between devices, on_device(): lax.ppermute(tiles[hop], 'grp', [(i, (i + hop) % 4) for i in range(4)])  4.51 us
    ppermute x3, starting transfers between devices, on_device(): lax.ppermute(tiles[hop], 'grp', [(i, (i + hop) % 4) for i in range(4)])  3.59 us
    pallas_call x1, Pallas kernels, convolve(): pl.pallas_call(conv_kernel, out_shape=jax.ShapeDtypeStruct((3, 1, TH * TW...  2.06 us
    pallas_call x1, Pallas kernels, plan(): pl.pallas_call(plan_kernel, out_shape=[jax.ShapeDtypeStruct((n,), jnp.int...  1.77 us
    pallas_call x1, Pallas kernels, pick(): pl.pallas_call(functools.partial(pick_kernel, capacity), out_shape=jax.Sh...  1.66 us
    unnamed x5, local copies, waits for them, and re-layouts  1.38 us
  transfers between devices with their start and end apart: 4, of which 2 were waited for; matrix products, arithmetic and copies ran while one was open for 4% of the time, Pallas kernels for 4%

profile of v1, /device:TPU:6, one launch (start us, length us, event | category | flops | bytes accessed | tf_op | source)
XLA Modules:
  0.0 45.2 jit_solution(12046366097659827743)
XLA Ops:
  0.0 0.0 collective-permute-start
  0.0 1.4 %copy.17 = bf16[1,15,73,384]{3,2,1,0:T(8,128)(2,1)S(1)} copy(bf16[1,15,73,384]{3,1,2,0:T(8,128)(2,1)} %param.11) | data formatting | bytes 1681920 | tf_op args[0]
  1.4 1.8 %plan.1 = (s32[128]{0:T(128)S(1)}, s32[1]{0:T(128)}) custom-call(s32[12]{0:T(128)} %lat.1, s32[12]{0:T(128)} %lon.1, s32[12]{0:T(128)} %order.1), custom_call_target="tpu_custom_call" | custom-call | tf_op jit(solution)/shard_map/plan/pallas_call | solution.py:98
  3.8 0.0 collective-permute-done
  3.8 0.0 copy-start
  3.8 0.0 copy-start.1
  3.8 30.3 %conditional.1 = ((bf16[144,128]{1,0:T(8,128)(2,1)S(1)}, bf16[144,128]{1,0:T(8,128)(2,1)S(1)}, bf16[144,128]{1,0:T(8,128)(2,1)S(1)}, bf16[144,128]{1,0:T(8,128)(2,1)S(1)})) conditional(s32[]{:T(128)} %bitcast, (s32[128]{0:T(128)S(1)}, bf16[15,73,384]{2,1,0:T(8,128)(2,1)S(1)}, ...), branch_computations={%region_0.0_spmd, %region_1.0_spmd, %region_2.0_spmd, %region_3.0_... | conditional | bytes 7186952 | solution.py:334
  3.9 0.2 copy.11.other
  4.1 1.7 %pick.6 = bf16[32,56,128]{2,1,0:T(8,128)(2,1)S(1)} custom-call(s32[128]{0:T(128)S(1)} %get-tuple-element.38.tables, bf16[15,73,384]{2,1,0:T(8,128)(2,1)S(1)} %get-tuple-element.39.own, bf16[15,73,384]{2,1,0:T(8,128)(2,1)S(1)} %copy.11.other), custom_call_target="tpu_custom_call" | custom-call | tf_op jit(solution)/shard_map/cond/branch_1_fun/pick/pallas_call | solution.py:194
  5.7 27.4 %all_to_all.21.got = bf16[32,56,128]{2,1,0:T(8,128)(2,1)S(1)} all-to-all(bf16[32,56,128]{2,1,0:T(8,128)(2,1)S(1)} %pick.6), channel_id=1, replica_groups={{0,8,16,24,32,40,48,56,64,72,80,88,96,104,112,120,128,136,144,152,160,1..., dimensions={0} | all-to-all | bytes 917504 | tf_op jit(solution)/shard_map/cond/branch_1_fun/all_to_all | solution.py:329
  33.1 0.8 %regroup.6 = (bf16[144,128]{1,0:T(8,128)(2,1)S(1)}, bf16[144,128]{1,0:T(8,128)(2,1)S(1)}, bf16[144,128]{1,0:T(8,128)(2,1)S(1)}, bf16[144,128]{1,0:T(8,128)(2,1)S(1)}) custom-call(s32[128]{0:T(128)S(1)} %get-tuple-element.38.tables, bf16[32,56,128]{2,1,0:T(8,128)(2,1)S(1)} %all_to_all.21.got), custom_call_target="tpu_custom_call" | custom-call | tf_op jit(solution)/shard_map/cond/branch_1_fun/regroup/pallas_call | solution.py:244
  34.2 1.5 %collective-permute-start.1 = (bf16[144,128]{1,0:T(8,128)(2,1)S(1)}, bf16[144,128]{1,0:T(8,128)(2,1)S(1)}, u32[]{:S(2)}, u32[]{:S(2)}) collective-permute-start(bf16[144,128]{1,0:T(8,128)(2,1)S(1)} %get-tuple-element.68), channel_id=1, source_target_pairs={{0,2},{1,3},{2,0},{3,1},{4,6},{5,7},{6,4},{7,5},{8,10},{9,11},{10,... | collective-permute-start | bytes 110600 | tf_op jit(solution)/shard_map/ppermute | solution.py:337
  35.7 2.1 %collective-permute-start.2 = (bf16[144,128]{1,0:T(8,128)(2,1)S(1)}, bf16[144,128]{1,0:T(8,128)(2,1)S(1)}, u32[]{:S(2)}, u32[]{:S(2)}) collective-permute-start(bf16[144,128]{1,0:T(8,128)(2,1)S(1)} %get-tuple-element.69), channel_id=1, source_target_pairs={{0,1},{1,2},{2,3},{3,0},{4,5},{5,6},{6,7},{7,4},{8,9},{9,10},{10,1... | collective-permute-start | bytes 110600 | tf_op jit(solution)/shard_map/ppermute | solution.py:337
  37.8 0.0 collective-permute-start.3
  37.9 0.1 maximum_select_fusion.1
  38.0 0.5 %multiply_convert_fusion = bf16[56,56,256]{2,1,0:T(8,128)(2,1)S(1)} fusion(f32[56,256]{1,0:T(8,128)S(1)} %maximum_select_fusion, f32[56,256]{1,0:T(8,128)S(1)} %maximum_select_fusion.1), kind=kLoop, calls=%fused_computation | loop fusion | flops 1605632 | bytes 1720320 | tf_op jit(solution)/shard_map/convert_element_type | solution.py:315
  38.5 1.4 %collective-permute-done.1.win1 = bf16[144,128]{1,0:T(8,128)(2,1)S(1)} collective-permute-done((bf16[144,128]{1,0:T(8,128)(2,1)S(1)}, bf16[144,128]{1,0:T(8,128)(2,1)S(1)}, u32[]{:S(2)}, u32[]{:S(2)}) %collective-permute-start.1) | collective-permute-done | bytes 36896 | tf_op jit(solution)/shard_map/ppermute | solution.py:337
  39.9 0.0 collective-permute-done.2.win2
  39.9 3.1 %collective-permute-done.3.win3 = bf16[144,128]{1,0:T(8,128)(2,1)S(1)} collective-permute-done((bf16[144,128]{1,0:T(8,128)(2,1)S(1)}, bf16[144,128]{1,0:T(8,128)(2,1)S(1)}, u32[]{:S(2)}, u32[]{:S(2)}) %collective-permute-start.3) | collective-permute-done | bytes 36896 | tf_op jit(solution)/shard_map/ppermute | solution.py:337
  43.0 0.0 copy-done
  43.0 0.0 copy-done.1
  43.0 2.1 %convolve.1 = bf16[3,1,3136,128]{3,2,1,0:T(8,128)(2,1)} custom-call(bf16[144,128]{1,0:T(8,128)(2,1)S(1)} %get-tuple-element.67.win0, bf16[144,128]{1,0:T(8,128)(2,1)S(1)} %collective-permute-done.1.win1, bf16[144,128]{1,0:T(8,128)(2,1)S(1)} %collective-permute-done.2.win2, bf16[144,128]{1,0:T(8,128)(2,1)S(1)} %collective-permute-done.3.win3, ...), custom_call_target="tpu_custom_call" | custom-call | tf_op jit(solution)/shard_map/convolve/pallas_call | solution.py:291
  (4 shorter events, 0.1 us)
Async XLA Ops:
  0.0 3.8 %collective-permute-start = (bf16[15,73,384]{2,0,1:T(8,128)(2,1)}, bf16[15,73,384]{2,0,1:T(8,128)(2,1)S(1)}, u32[]{:S(2)}, u32[]{:S(2)}) collective-permute-start(bf16[15,73,384]{2,0,1:T(8,128)(2,1)} %bitcast.17), channel_id=1, source_target_pairs={{0,4},{4,0},{8,12},{12,8},{16,20},{20,16},{24,28},{28,24},{32,36},... | collective-permute-start | bytes 2522888 | tf_op jit(solution)/shard_map/ppermute | solution.py:321
  3.8 39.2 %copy-start = (bf16[9,128,73]{1,2,0:T(8,128)(2,1)S(1)}, bf16[9,128,73]{1,2,0:T(8,128)(2,1)}, u32[]{:S(2)}) copy-start(bf16[9,128,73]{1,2,0:T(8,128)(2,1)} %param.15) | copy-start | bytes 504580
  3.8 39.2 %copy-start.1 = (f32[128]{0:T(128)S(1)}, f32[128]{0:T(128)}, u32[]{:S(2)}) copy-start(f32[128]{0:T(128)} %param.16) | copy-start | bytes 1540
  34.2 5.6 %collective-permute-start.1 = (bf16[144,128]{1,0:T(8,128)(2,1)S(1)}, bf16[144,128]{1,0:T(8,128)(2,1)S(1)}, u32[]{:S(2)}, u32[]{:S(2)}) collective-permute-start(bf16[144,128]{1,0:T(8,128)(2,1)S(1)} %get-tuple-element.68), channel_id=1, source_target_pairs={{0,2},{1,3},{2,0},{3,1},{4,6},{5,7},{6,4},{7,5},{8,10},{9,11},{10,... | collective-permute-start | bytes 110600 | tf_op jit(solution)/shard_map/ppermute | solution.py:337
  35.7 4.1 %collective-permute-start.2 = (bf16[144,128]{1,0:T(8,128)(2,1)S(1)}, bf16[144,128]{1,0:T(8,128)(2,1)S(1)}, u32[]{:S(2)}, u32[]{:S(2)}) collective-permute-start(bf16[144,128]{1,0:T(8,128)(2,1)S(1)} %get-tuple-element.69), channel_id=1, source_target_pairs={{0,1},{1,2},{2,3},{3,0},{4,5},{5,6},{6,7},{7,4},{8,9},{9,10},{10,1... | collective-permute-start | bytes 110600 | tf_op jit(solution)/shard_map/ppermute | solution.py:337
  37.8 5.2 %collective-permute-start.3 = (bf16[144,128]{1,0:T(8,128)(2,1)S(1)}, bf16[144,128]{1,0:T(8,128)(2,1)S(1)}, u32[]{:S(2)}, u32[]{:S(2)}) collective-permute-start(bf16[144,128]{1,0:T(8,128)(2,1)S(1)} %get-tuple-element.70), channel_id=1, source_target_pairs={{0,3},{1,0},{2,1},{3,2},{4,7},{5,4},{6,5},{7,6},{8,11},{9,8},{10,9... | collective-permute-start | bytes 110600 | tf_op jit(solution)/shard_map/ppermute | solution.py:337

commit v2 on v1

--- a/solution.py
+++ b/solution.py
@@ -42,7 +42,14 @@
     return jnp.where(inside, weight, 0.0)
 
 
-def plan_kernel(lat, lon, order, tables, branch, counts):
+def plan_kernel(lat, lon, order, held_rows, tables, branch, near_rows, counts, sems):
+    fetches = []
+    for n, first in enumerate(range(0, CH, 10)):
+        part = pl.ds(first, min(10, CH - first))
+        fetches.append(
+            pltpu.make_async_copy(held_rows.at[part], near_rows.at[part], sems.at[n])
+        )
+        fetches[-1].start()
     band, group = lax.axis_index("band"), lax.axis_index("grp")
     chip, core = lax.shift_right_logical(band, 1), lax.bitwise_and(band, 1)
     spot = lax.broadcasted_iota(jnp.int32, (8, 128), 1)
@@ -91,18 +98,21 @@
                 tables[at + 2 * j + k] = jnp.where(ok, side + col, -1)
         q = q + mine.astype(jnp.int32)
     tables[HELD] = q
-
-
-def plan(lat, lon, order):
+    for fetch in fetches:
+        fetch.wait()
+
+
+def plan(lat, lon, order, held_rows):
     smem = pl.BlockSpec(memory_space=pltpu.SMEM)
     return pl.pallas_call(
         plan_kernel,
-        out_shape=[jax.ShapeDtypeStruct((n,), jnp.int32) for n in (128, 1)],
-        in_specs=[smem] * 3,
-        out_specs=[smem] * 2,
-        scratch_shapes=[pltpu.SMEM((33,), jnp.int32)],
+        out_shape=[jax.ShapeDtypeStruct((n,), jnp.int32) for n in (128, 1)]
+        + [pltpu.VMEM(held_rows.shape, held_rows.dtype)],
+        in_specs=[smem] * 3 + [pl.BlockSpec(memory_space=pl.ANY)],
+        out_specs=[smem] * 2 + [pl.BlockSpec(memory_space=pltpu.VMEM)],
+        scratch_shapes=[pltpu.SMEM((33,), jnp.int32), pltpu.SemaphoreType.DMA((8,))],
         name="plan",
-    )(lat, lon, order)
+    )(lat, lon, order, held_rows)
 
 
 def payload_rows(capacity):
@@ -319,8 +329,10 @@
     band = lax.axis_index("band")
     own = coarse[0]
     other = lax.ppermute(own, "band", [(i, i ^ 1) for i in range(64)])
-    own = with_layout_constraint(own, Layout(major_to_minor=(0, 1, 2)))
-    tables, branch = plan(region_lat, region_lon, region_order)
+    tables, branch, own = plan(
+        region_lat, region_lon, region_order, jnp.swapaxes(own, 0, 1)
+    )
+    own = with_layout_constraint(jnp.swapaxes(own, 0, 1), Layout(major_to_minor=(0, 1, 2)))
     planes = [[2 * m + c for m in range(32)] for c in range(2)]
 
     def route(capacity):

time: 46 us -> 45.8 us (level)
  local copies, waits for them, and re-layouts: 1.57 us -> 0.4 us
  Pallas kernels: 6.27 us -> 7.31 us
    unnamed x5 -> x4, local copies, waits for them, and re-layouts: 1.38 us -> 0.01 us
    pallas_call x1, Pallas kernels: 1.77 us -> 2.81 us  [plan(): pl.pallas_call(plan_kernel, out_shape=[jax.ShapeDtypeStruct((n,), jnp.int...]
  transfers between devices with their start and end apart: 4 -> 4, of which waited for: 2 -> 2; matrix products, arithmetic and copies ran while one was open for 4% -> 2% of each run, Pallas kernels for 4% -> 6%
where the time goes in v2:
time: 45.8 us; the launch traced here: 45.1 us
  blocking collectives  27.4 us (60%)
  Pallas kernels  7.31 us (16%)
  waiting for transfers between devices  4.51 us (10%)
  starting transfers between devices  3.6 us (8%)
  between operations  0.95 us (2%)
  other arithmetic  0.67 us (1%)
    all_to_all x1, blocking collectives, run(): got = lax.all_to_all(cut, 'band', 0, 0, axis_index_groups=planes)  27.4 us
    ppermute x3, waiting for transfers between devices, on_device(): lax.ppermute(tiles[hop], 'grp', [(i, (i + hop) % 4) for i in range(4)])  4.51 us
    ppermute x3, starting transfers between devices, on_device(): lax.ppermute(tiles[hop], 'grp', [(i, (i + hop) % 4) for i in range(4)])  3.59 us
    pallas_call x1, Pallas kernels, plan(): pl.pallas_call(plan_kernel, out_shape=[jax.ShapeDtypeStruct((n,), jnp.int...  2.81 us
    pallas_call x1, Pallas kernels, convolve(): pl.pallas_call(conv_kernel, out_shape=jax.ShapeDtypeStruct((3, 1, TH * TW...  2.06 us
    pallas_call x1, Pallas kernels, pick(): pl.pallas_call(functools.partial(pick_kernel, capacity), out_shape=jax.Sh...  1.66 us
  transfers between devices with their start and end apart: 4, of which 2 were waited for; matrix products, arithmetic and copies ran while one was open for 2% of the time, Pallas kernels for 6%

profile of v2, /device:TPU:6, one launch (start us, length us, event | category | flops | bytes accessed | tf_op | source)
XLA Modules:
  0.0 45.1 jit_solution(7309212743673858194)
XLA Ops:
  0.0 0.0 collective-permute-start
  0.0 2.8 %plan.1 = (s32[128]{0:T(128)S(1)}, s32[1]{0:T(128)}, bf16[73,15,384]{2,1,0:T(8,128)(2,1)S(1)}) custom-call(s32[12]{0:T(128)} %lat.1, s32[12]{0:T(128)} %lon.1, s32[12]{0:T(128)} %order.1, bf16[73,15,384]{2,1,0:T(8,128)(2,1)} %bitcast.20), custom_call_target="tpu_custom_call" | custom-call | tf_op jit(solution)/shard_map/plan/pallas_call | solution.py:107
  2.8 0.2 copy.14
  3.7 0.0 collective-permute-done
  3.7 0.0 copy-start
  3.7 0.0 copy-start.1
  3.7 30.3 %conditional.1 = ((bf16[144,128]{1,0:T(8,128)(2,1)S(1)}, bf16[144,128]{1,0:T(8,128)(2,1)S(1)}, bf16[144,128]{1,0:T(8,128)(2,1)S(1)}, bf16[144,128]{1,0:T(8,128)(2,1)S(1)})) conditional(s32[]{:T(128)} %bitcast.2, (s32[128]{0:T(128)S(1)}, bf16[15,73,384]{2,1,0:T(8,128)(2,1)S(1)}, ...), branch_computations={%region_0.0_spmd, %region_1.0_spmd, %region_2.0_spmd, %region_3.0_... | conditional | bytes 7186952 | solution.py:346
  3.7 0.2 copy.9.other
  3.9 1.7 %pick.6 = bf16[32,56,128]{2,1,0:T(8,128)(2,1)S(1)} custom-call(s32[128]{0:T(128)S(1)} %get-tuple-element.38.tables, bf16[15,73,384]{2,1,0:T(8,128)(2,1)S(1)} %get-tuple-element.39.own, bf16[15,73,384]{2,1,0:T(8,128)(2,1)S(1)} %copy.9.other), custom_call_target="tpu_custom_call" | custom-call | tf_op jit(solution)/shard_map/cond/branch_1_fun/pick/pallas_call | solution.py:204
  5.6 27.4 %all_to_all.21.got = bf16[32,56,128]{2,1,0:T(8,128)(2,1)S(1)} all-to-all(bf16[32,56,128]{2,1,0:T(8,128)(2,1)S(1)} %pick.6), channel_id=1, replica_groups={{0,8,16,24,32,40,48,56,64,72,80,88,96,104,112,120,128,136,144,152,160,1..., dimensions={0} | all-to-all | bytes 917504 | tf_op jit(solution)/shard_map/cond/branch_1_fun/all_to_all | solution.py:341
  33.0 0.8 %regroup.6 = (bf16[144,128]{1,0:T(8,128)(2,1)S(1)}, bf16[144,128]{1,0:T(8,128)(2,1)S(1)}, bf16[144,128]{1,0:T(8,128)(2,1)S(1)}, bf16[144,128]{1,0:T(8,128)(2,1)S(1)}) custom-call(s32[128]{0:T(128)S(1)} %get-tuple-element.38.tables, bf16[32,56,128]{2,1,0:T(8,128)(2,1)S(1)} %all_to_all.21.got), custom_call_target="tpu_custom_call" | custom-call | tf_op jit(solution)/shard_map/cond/branch_1_fun/regroup/pallas_call | solution.py:254
  34.1 1.5 %collective-permute-start.1 = (bf16[144,128]{1,0:T(8,128)(2,1)S(1)}, bf16[144,128]{1,0:T(8,128)(2,1)S(1)}, u32[]{:S(2)}, u32[]{:S(2)}) collective-permute-start(bf16[144,128]{1,0:T(8,128)(2,1)S(1)} %get-tuple-element.70), channel_id=1, source_target_pairs={{0,2},{1,3},{2,0},{3,1},{4,6},{5,7},{6,4},{7,5},{8,10},{9,11},{10,... | collective-permute-start | bytes 110600 | tf_op jit(solution)/shard_map/ppermute | solution.py:349
  35.6 2.1 %collective-permute-start.2 = (bf16[144,128]{1,0:T(8,128)(2,1)S(1)}, bf16[144,128]{1,0:T(8,128)(2,1)S(1)}, u32[]{:S(2)}, u32[]{:S(2)}) collective-permute-start(bf16[144,128]{1,0:T(8,128)(2,1)S(1)} %get-tuple-element.71), channel_id=1, source_target_pairs={{0,1},{1,2},{2,3},{3,0},{4,5},{5,6},{6,7},{7,4},{8,9},{9,10},{10,1... | collective-permute-start | bytes 110600 | tf_op jit(solution)/shard_map/ppermute | solution.py:349
  37.7 0.0 collective-permute-start.3
  37.8 0.1 maximum_select_fusion.1
  37.9 0.5 %multiply_convert_fusion = bf16[56,56,256]{2,1,0:T(8,128)(2,1)S(1)} fusion(f32[56,256]{1,0:T(8,128)S(1)} %maximum_select_fusion, f32[56,256]{1,0:T(8,128)S(1)} %maximum_select_fusion.1), kind=kLoop, calls=%fused_computation | loop fusion | flops 1605632 | bytes 1720320 | tf_op jit(solution)/shard_map/convert_element_type | solution.py:325
  38.4 1.4 %collective-permute-done.1.win1 = bf16[144,128]{1,0:T(8,128)(2,1)S(1)} collective-permute-done((bf16[144,128]{1,0:T(8,128)(2,1)S(1)}, bf16[144,128]{1,0:T(8,128)(2,1)S(1)}, u32[]{:S(2)}, u32[]{:S(2)}) %collective-permute-start.1) | collective-permute-done | bytes 36896 | tf_op jit(solution)/shard_map/ppermute | solution.py:349
  39.7 0.0 collective-permute-done.2.win2
  39.7 3.1 %collective-permute-done.3.win3 = bf16[144,128]{1,0:T(8,128)(2,1)S(1)} collective-permute-done((bf16[144,128]{1,0:T(8,128)(2,1)S(1)}, bf16[144,128]{1,0:T(8,128)(2,1)S(1)}, u32[]{:S(2)}, u32[]{:S(2)}) %collective-permute-start.3) | collective-permute-done | bytes 36896 | tf_op jit(solution)/shard_map/ppermute | solution.py:349
  42.9 0.0 copy-done
  42.9 0.0 copy-done.1
  42.9 2.1 %convolve.1 = bf16[3,1,3136,128]{3,2,1,0:T(8,128)(2,1)} custom-call(bf16[144,128]{1,0:T(8,128)(2,1)S(1)} %get-tuple-element.69.win0, bf16[144,128]{1,0:T(8,128)(2,1)S(1)} %collective-permute-done.1.win1, bf16[144,128]{1,0:T(8,128)(2,1)S(1)} %collective-permute-done.2.win2, bf16[144,128]{1,0:T(8,128)(2,1)S(1)} %collective-permute-done.3.win3, ...), custom_call_target="tpu_custom_call" | custom-call | tf_op jit(solution)/shard_map/convolve/pallas_call | solution.py:301
  (4 shorter events, 0.1 us)
Async XLA Ops:
  0.0 3.7 %collective-permute-start = (bf16[15,73,384]{2,0,1:T(8,128)(2,1)}, bf16[15,73,384]{2,0,1:T(8,128)(2,1)S(1)}, u32[]{:S(2)}, u32[]{:S(2)}) collective-permute-start(bf16[15,73,384]{2,0,1:T(8,128)(2,1)} %bitcast.19), channel_id=1, source_target_pairs={{0,4},{4,0},{8,12},{12,8},{16,20},{20,16},{24,28},{28,24},{32,36},... | collective-permute-start | bytes 2522888 | tf_op jit(solution)/shard_map/ppermute | solution.py:331
  3.7 39.2 %copy-start = (bf16[9,128,73]{1,2,0:T(8,128)(2,1)S(1)}, bf16[9,128,73]{1,2,0:T(8,128)(2,1)}, u32[]{:S(2)}) copy-start(bf16[9,128,73]{1,2,0:T(8,128)(2,1)} %param.15) | copy-start | bytes 504580
  3.7 39.2 %copy-start.1 = (f32[128]{0:T(128)S(1)}, f32[128]{0:T(128)}, u32[]{:S(2)}) copy-start(f32[128]{0:T(128)} %param.16) | copy-start | bytes 1540
  34.1 5.6 %collective-permute-start.1 = (bf16[144,128]{1,0:T(8,128)(2,1)S(1)}, bf16[144,128]{1,0:T(8,128)(2,1)S(1)}, u32[]{:S(2)}, u32[]{:S(2)}) collective-permute-start(bf16[144,128]{1,0:T(8,128)(2,1)S(1)} %get-tuple-element.70), channel_id=1, source_target_pairs={{0,2},{1,3},{2,0},{3,1},{4,6},{5,7},{6,4},{7,5},{8,10},{9,11},{10,... | collective-permute-start | bytes 110600 | tf_op jit(solution)/shard_map/ppermute | solution.py:349
  35.6 4.1 %collective-permute-start.2 = (bf16[144,128]{1,0:T(8,128)(2,1)S(1)}, bf16[144,128]{1,0:T(8,128)(2,1)S(1)}, u32[]{:S(2)}, u32[]{:S(2)}) collective-permute-start(bf16[144,128]{1,0:T(8,128)(2,1)S(1)} %get-tuple-element.71), channel_id=1, source_target_pairs={{0,1},{1,2},{2,3},{3,0},{4,5},{5,6},{6,7},{7,4},{8,9},{9,10},{10,1... | collective-permute-start | bytes 110600 | tf_op jit(solution)/shard_map/ppermute | solution.py:349
  37.7 5.2 %collective-permute-start.3 = (bf16[144,128]{1,0:T(8,128)(2,1)S(1)}, bf16[144,128]{1,0:T(8,128)(2,1)S(1)}, u32[]{:S(2)}, u32[]{:S(2)}) collective-permute-start(bf16[144,128]{1,0:T(8,128)(2,1)S(1)} %get-tuple-element.72), channel_id=1, source_target_pairs={{0,3},{1,0},{2,1},{3,2},{4,7},{5,4},{6,5},{7,6},{8,11},{9,8},{10,9... | collective-permute-start | bytes 110600 | tf_op jit(solution)/shard_map/ppermute | solution.py:349

commit v3 on v2

--- a/solution.py
+++ b/solution.py
@@ -40,6 +40,10 @@
     weight = jnp.maximum(0.0, 1.0 - jnp.abs(coords - nodes.astype(F32)))
     inside = (positions >= 0) & (positions < fine_count)
     return jnp.where(inside, weight, 0.0)
+
+
+def rank_of(chip):
+    return lax.bitwise_and(chip, 7) * 4 + lax.shift_right_logical(chip, 3)
 
 
 def plan_kernel(lat, lon, order, held_rows, tables, branch, near_rows, counts, sems):
@@ -69,8 +73,8 @@
         tally = tally + meets.astype(jnp.int32)
         counts[m0] = 0
         counts[m1] = 0
-        tables[CHIPS + 2 * i] = m0
-        tables[CHIPS + 2 * i + 1] = m1
+        tables[CHIPS + 2 * i] = rank_of(m0)
+        tables[CHIPS + 2 * i + 1] = rank_of(m1)
         held.append((lat0, lon0, lon1, m0, m1, (g0 == group) | (g1 == group)))
     most = jnp.max(tally)
     step = jnp.int32(0)
@@ -192,7 +196,8 @@
                     rests.append(rest)
                 else:
                     rests[-1] = rests[-1] + rest
-            out[4 * a + b] = jnp.concatenate(mains + rests, axis=0).astype(BF16)
+            chip = 4 * a + b
+            out[rank_of(chip)] = jnp.concatenate(mains + rests, axis=0).astype(BF16)
         return carry
 
     lax.fori_loop(0, 8, emit, 0, unroll=8 if capacity <= 2 else 1)
@@ -333,7 +338,7 @@
         region_lat, region_lon, region_order, jnp.swapaxes(own, 0, 1)
     )
     own = with_layout_constraint(jnp.swapaxes(own, 0, 1), Layout(major_to_minor=(0, 1, 2)))
-    planes = [[2 * m + c for m in range(32)] for c in range(2)]
+    planes = [[2 * (8 * y + z) + c for z in range(8) for y in range(4)] for c in range(2)]
 
     def route(capacity):
         def run(own, other, tables):

time: 45.8 us -> 46.3 us (1.011); the launches traced: 45.1 us -> 46.2 us
  blocking collectives: 27.4 us -> 28.5 us
    all_to_all x1, blocking collectives: 27.4 us -> 28.5 us  [run(): got = lax.all_to_all(cut, 'band', 0, 0, axis_index_groups=planes)]
where the time goes in v3:
time: 46.3 us; the launch traced here: 46.2 us
  blocking collectives  28.5 us (62%)
  Pallas kernels  7.33 us (16%)
  waiting for transfers between devices  4.51 us (10%)
  starting transfers between devices  3.6 us (8%)
  between operations  0.95 us (2%)
  other arithmetic  0.67 us (1%)
    all_to_all x1, blocking collectives, run(): got = lax.all_to_all(cut, 'band', 0, 0, axis_index_groups=planes)  28.5 us
    ppermute x3, waiting for transfers between devices, on_device(): lax.ppermute(tiles[hop], 'grp', [(i, (i + hop) % 4) for i in range(4)])  4.51 us
    ppermute x3, starting transfers between devices, on_device(): lax.ppermute(tiles[hop], 'grp', [(i, (i + hop) % 4) for i in range(4)])  3.59 us
    pallas_call x1, Pallas kernels, plan(): pl.pallas_call(plan_kernel, out_shape=[jax.ShapeDtypeStruct((n,), jnp.int...  2.81 us
    pallas_call x1, Pallas kernels, convolve(): pl.pallas_call(conv_kernel, out_shape=jax.ShapeDtypeStruct((3, 1, TH * TW...  2.07 us
    pallas_call x1, Pallas kernels, pick(): pl.pallas_call(functools.partial(pick_kernel, capacity), out_shape=jax.Sh...  1.67 us
  transfers between devices with their start and end apart: 4, of which 2 were waited for; matrix products, arithmetic and copies ran while one was open for 2% of the time, Pallas kernels for 6%

profile of v3, /device:TPU:6, one launch (start us, length us, event | category | flops | bytes accessed | tf_op | source)
XLA Modules:
  0.0 46.2 jit_solution(3618540052082262201)
XLA Ops:
  0.0 0.0 collective-permute-start
  0.0 2.8 %plan.1 = (s32[128]{0:T(128)S(1)}, s32[1]{0:T(128)}, bf16[73,15,384]{2,1,0:T(8,128)(2,1)S(1)}) custom-call(s32[12]{0:T(128)} %lat.1, s32[12]{0:T(128)} %lon.1, s32[12]{0:T(128)} %order.1, bf16[73,15,384]{2,1,0:T(8,128)(2,1)} %bitcast.20), custom_call_target="tpu_custom_call" | custom-call | tf_op jit(solution)/shard_map/plan/pallas_call | solution.py:111
  2.8 0.2 copy.14
  3.7 0.0 collective-permute-done
  3.7 0.0 copy-start
  3.7 0.0 copy-start.1
  3.7 31.4 %conditional.1 = ((bf16[144,128]{1,0:T(8,128)(2,1)S(1)}, bf16[144,128]{1,0:T(8,128)(2,1)S(1)}, bf16[144,128]{1,0:T(8,128)(2,1)S(1)}, bf16[144,128]{1,0:T(8,128)(2,1)S(1)})) conditional(s32[]{:T(128)} %bitcast.2, (s32[128]{0:T(128)S(1)}, bf16[15,73,384]{2,1,0:T(8,128)(2,1)S(1)}, ...), branch_computations={%region_0.0_spmd, %region_1.0_spmd, %region_2.0_spmd, %region_3.0_... | conditional | bytes 7186952 | solution.py:351
  3.7 0.2 copy.9.other
  3.9 1.7 %pick.6 = bf16[32,56,128]{2,1,0:T(8,128)(2,1)S(1)} custom-call(s32[128]{0:T(128)S(1)} %get-tuple-element.38.tables, bf16[15,73,384]{2,1,0:T(8,128)(2,1)S(1)} %get-tuple-element.39.own, bf16[15,73,384]{2,1,0:T(8,128)(2,1)S(1)} %copy.9.other), custom_call_target="tpu_custom_call" | custom-call | tf_op jit(solution)/shard_map/cond/branch_1_fun/pick/pallas_call | solution.py:209
  5.6 28.5 %all_to_all.21.got = bf16[32,56,128]{2,1,0:T(8,128)(2,1)S(1)} all-to-all(bf16[32,56,128]{2,1,0:T(8,128)(2,1)S(1)} %pick.6), channel_id=1, replica_groups={{0,64,128,192,8,72,136,200,16,80,144,208,24,88,152,216,32,96,160,224,40..., dimensions={0} | all-to-all | bytes 917504 | tf_op jit(solution)/shard_map/cond/branch_1_fun/all_to_all | solution.py:346
  34.1 0.8 %regroup.6 = (bf16[144,128]{1,0:T(8,128)(2,1)S(1)}, bf16[144,128]{1,0:T(8,128)(2,1)S(1)}, bf16[144,128]{1,0:T(8,128)(2,1)S(1)}, bf16[144,128]{1,0:T(8,128)(2,1)S(1)}) custom-call(s32[128]{0:T(128)S(1)} %get-tuple-element.38.tables, bf16[32,56,128]{2,1,0:T(8,128)(2,1)S(1)} %all_to_all.21.got), custom_call_target="tpu_custom_call" | custom-call | tf_op jit(solution)/shard_map/cond/branch_1_fun/regroup/pallas_call | solution.py:259
  35.2 1.5 %collective-permute-start.1 = (bf16[144,128]{1,0:T(8,128)(2,1)S(1)}, bf16[144,128]{1,0:T(8,128)(2,1)S(1)}, u32[]{:S(2)}, u32[]{:S(2)}) collective-permute-start(bf16[144,128]{1,0:T(8,128)(2,1)S(1)} %get-tuple-element.70), channel_id=1, source_target_pairs={{0,2},{1,3},{2,0},{3,1},{4,6},{5,7},{6,4},{7,5},{8,10},{9,11},{10,... | collective-permute-start | bytes 110600 | tf_op jit(solution)/shard_map/ppermute | solution.py:354
  36.7 2.1 %collective-permute-start.2 = (bf16[144,128]{1,0:T(8,128)(2,1)S(1)}, bf16[144,128]{1,0:T(8,128)(2,1)S(1)}, u32[]{:S(2)}, u32[]{:S(2)}) collective-permute-start(bf16[144,128]{1,0:T(8,128)(2,1)S(1)} %get-tuple-element.71), channel_id=1, source_target_pairs={{0,1},{1,2},{2,3},{3,0},{4,5},{5,6},{6,7},{7,4},{8,9},{9,10},{10,1... | collective-permute-start | bytes 110600 | tf_op jit(solution)/shard_map/ppermute | solution.py:354
  38.8 0.0 collective-permute-start.3
  38.8 0.1 maximum_select_fusion.1
  38.9 0.5 %multiply_convert_fusion = bf16[56,56,256]{2,1,0:T(8,128)(2,1)S(1)} fusion(f32[56,256]{1,0:T(8,128)S(1)} %maximum_select_fusion, f32[56,256]{1,0:T(8,128)S(1)} %maximum_select_fusion.1), kind=kLoop, calls=%fused_computation | loop fusion | flops 1605632 | bytes 1720320 | tf_op jit(solution)/shard_map/convert_element_type | solution.py:330
  39.4 1.3 %collective-permute-done.1.win1 = bf16[144,128]{1,0:T(8,128)(2,1)S(1)} collective-permute-done((bf16[144,128]{1,0:T(8,128)(2,1)S(1)}, bf16[144,128]{1,0:T(8,128)(2,1)S(1)}, u32[]{:S(2)}, u32[]{:S(2)}) %collective-permute-start.1) | collective-permute-done | bytes 36896 | tf_op jit(solution)/shard_map/ppermute | solution.py:354
  40.7 0.0 collective-permute-done.2.win2
  40.7 3.2 %collective-permute-done.3.win3 = bf16[144,128]{1,0:T(8,128)(2,1)S(1)} collective-permute-done((bf16[144,128]{1,0:T(8,128)(2,1)S(1)}, bf16[144,128]{1,0:T(8,128)(2,1)S(1)}, u32[]{:S(2)}, u32[]{:S(2)}) %collective-permute-start.3) | collective-permute-done | bytes 36896 | tf_op jit(solution)/shard_map/ppermute | solution.py:354
  43.9 0.0 copy-done
  43.9 0.0 copy-done.1
  43.9 2.1 %convolve.1 = bf16[3,1,3136,128]{3,2,1,0:T(8,128)(2,1)} custom-call(bf16[144,128]{1,0:T(8,128)(2,1)S(1)} %get-tuple-element.69.win0, bf16[144,128]{1,0:T(8,128)(2,1)S(1)} %collective-permute-done.1.win1, bf16[144,128]{1,0:T(8,128)(2,1)S(1)} %collective-permute-done.2.win2, bf16[144,128]{1,0:T(8,128)(2,1)S(1)} %collective-permute-done.3.win3, ...), custom_call_target="tpu_custom_call" | custom-call | tf_op jit(solution)/shard_map/convolve/pallas_call | solution.py:306
  (4 shorter events, 0.1 us)
Async XLA Ops:
  0.0 3.7 %collective-permute-start = (bf16[15,73,384]{2,0,1:T(8,128)(2,1)}, bf16[15,73,384]{2,0,1:T(8,128)(2,1)S(1)}, u32[]{:S(2)}, u32[]{:S(2)}) collective-permute-start(bf16[15,73,384]{2,0,1:T(8,128)(2,1)} %bitcast.19), channel_id=1, source_target_pairs={{0,4},{4,0},{8,12},{12,8},{16,20},{20,16},{24,28},{28,24},{32,36},... | collective-permute-start | bytes 2522888 | tf_op jit(solution)/shard_map/ppermute | solution.py:336
  3.7 40.2 %copy-start = (bf16[9,128,73]{1,2,0:T(8,128)(2,1)S(1)}, bf16[9,128,73]{1,2,0:T(8,128)(2,1)}, u32[]{:S(2)}) copy-start(bf16[9,128,73]{1,2,0:T(8,128)(2,1)} %param.15) | copy-start | bytes 504580
  3.7 40.2 %copy-start.1 = (f32[128]{0:T(128)S(1)}, f32[128]{0:T(128)}, u32[]{:S(2)}) copy-start(f32[128]{0:T(128)} %param.16) | copy-start | bytes 1540
  35.2 5.6 %collective-permute-start.1 = (bf16[144,128]{1,0:T(8,128)(2,1)S(1)}, bf16[144,128]{1,0:T(8,128)(2,1)S(1)}, u32[]{:S(2)}, u32[]{:S(2)}) collective-permute-start(bf16[144,128]{1,0:T(8,128)(2,1)S(1)} %get-tuple-element.70), channel_id=1, source_target_pairs={{0,2},{1,3},{2,0},{3,1},{4,6},{5,7},{6,4},{7,5},{8,10},{9,11},{10,... | collective-permute-start | bytes 110600 | tf_op jit(solution)/shard_map/ppermute | solution.py:354
  36.7 4.1 %collective-permute-start.2 = (bf16[144,128]{1,0:T(8,128)(2,1)S(1)}, bf16[144,128]{1,0:T(8,128)(2,1)S(1)}, u32[]{:S(2)}, u32[]{:S(2)}) collective-permute-start(bf16[144,128]{1,0:T(8,128)(2,1)S(1)} %get-tuple-element.71), channel_id=1, source_target_pairs={{0,1},{1,2},{2,3},{3,0},{4,5},{5,6},{6,7},{7,4},{8,9},{9,10},{10,1... | collective-permute-start | bytes 110600 | tf_op jit(solution)/shard_map/ppermute | solution.py:354
  38.8 5.2 %collective-permute-start.3 = (bf16[144,128]{1,0:T(8,128)(2,1)S(1)}, bf16[144,128]{1,0:T(8,128)(2,1)S(1)}, u32[]{:S(2)}, u32[]{:S(2)}) collective-permute-start(bf16[144,128]{1,0:T(8,128)(2,1)S(1)} %get-tuple-element.72), channel_id=1, source_target_pairs={{0,3},{1,0},{2,1},{3,2},{4,7},{5,4},{6,5},{7,6},{8,11},{9,8},{10,9... | collective-permute-start | bytes 110600 | tf_op jit(solution)/shard_map/ppermute | solution.py:354
